TPU v7x, 32 devices: a whole 2x2x4 slice. The times are simulated.
32 devices in a mesh: seq: 2 (over x), dp: 4 (over z), fsdp: 4 (over y, core).
Axes of the slice: x: 2, y: 2, z: 4, core: 2. Of those that a mesh axis runs over, the one named last changes fastest.
Arguments:
- query_rows: bfloat16 [16, 256, 4096], P(('dp', 'fsdp'), 'seq'), may hold values from -2.5 to 2.5
- forward_key_rows: bfloat16 [16, 256, 1024], P(('dp', 'fsdp'), 'seq'), may hold values from -2.5 to 2.5
- forward_value_rows: bfloat16 [16, 256, 1024], P(('dp', 'fsdp'), 'seq'), may hold values from -4 to 4
- out_cotangent: bfloat16 [16, 256, 4096], P(('dp', 'fsdp'), 'seq'), may hold values from -4 to 4
- proj_weight: bfloat16 [4096, 4096], P(('dp', 'fsdp'), 'seq'), may hold values from -0.09375 to 0.09375
- sent_lengths: int32 [16, 8], P(('dp', 'fsdp')), may hold values from 1 to 64, 256 in all within a row
Outputs:
- query_grad: bfloat16 [16, 256, 4096], P(('dp', 'fsdp'), 'seq')
- key_gradient: bfloat16 [16, 256, 1024], P(('dp', 'fsdp'), 'seq')
- value_gradient: bfloat16 [16, 256, 1024], P(('dp', 'fsdp'), 'seq')
- proj_grad: bfloat16 [4096, 4096], P(('dp', 'fsdp'), 'seq')
Inputs may be any that keep to these rules, and one draw needn't show every extreme that they name: `sent_lengths`: each window's 8 lengths sum to 256, and the longest is exactly 64.
All inputs are finite; a program needn't handle non-finite values.
Results may differ from a plain program's by a relative error of at most 0.0058.
Values may be sent and summed in bfloat16 or wider, within the bound.
A program may use at most 128 MiB of HBM per device.

v0:
```python
import math

import jax
import jax.numpy as jnp
from jax import lax
from jax.sharding import PartitionSpec as P

QUERY_HEADS = 32
KEY_VALUE_HEADS = 8
HEAD_SIZE = 128


def per_device(
    query_rows, forward_key_rows, forward_value_rows, out_cotangent, proj_weight, sent_lengths
):
    queries_per_group = QUERY_HEADS // KEY_VALUE_HEADS
    factor = 1.0 / math.sqrt(HEAD_SIZE)
    gathered = lax.all_gather(out_cotangent, "seq", axis=1, tiled=True)
    cotangent = gathered[0]
    length = cotangent.shape[0]
    sliced = cotangent
    upstream_gradient = jnp.dot(
        sliced,
        lax.all_gather(proj_weight, ("dp", "fsdp"), axis=0, tiled=True),
        preferred_element_type=jnp.float32,
    ).astype(jnp.bfloat16)
    heads_of_queries, heads_of_keys, heads_of_values = (
        lax.all_to_all(query_rows, "seq", split_axis=2, concat_axis=1, tiled=True),
        lax.all_to_all(forward_key_rows, "seq", split_axis=2, concat_axis=1, tiled=True),
        lax.all_to_all(forward_value_rows, "seq", split_axis=2, concat_axis=1, tiled=True),
    )
    heads_of_queries = heads_of_queries[0]
    heads_of_keys = heads_of_keys[0]
    heads_of_values = heads_of_values[0]
    bounds = jnp.cumsum(sent_lengths[0])
    places = jnp.arange(length, dtype=jnp.int32)
    sentence = jnp.sum((places[:, None] >= bounds[None, :]).astype(jnp.int32), axis=1)
    block_rows = min(512, length)
    block_count = length // block_rows
    kv_local = heads_of_keys.shape[1] // HEAD_SIZE
    group_cols = queries_per_group * HEAD_SIZE
    output_parts = []
    query_parts = []
    key_parts = []
    value_parts = []
    for head_index in range(kv_local):
        key_head = heads_of_keys[:, head_index * HEAD_SIZE : (head_index + 1) * HEAD_SIZE]
        value_head = heads_of_values[:, head_index * HEAD_SIZE : (head_index + 1) * HEAD_SIZE]
        query_group = heads_of_queries[:, head_index * group_cols : (head_index + 1) * group_cols]
        upstream_group = upstream_gradient[
            :, head_index * group_cols : (head_index + 1) * group_cols
        ]

        def block_step(block_index, buffers):
            output_buf, query_buf, key_buf, value_buf = buffers
            offset = block_index * block_rows
            query_block = lax.dynamic_slice_in_dim(query_group, offset, block_rows, 0).reshape(
                block_rows, queries_per_group, HEAD_SIZE
            )
            upstream_block = lax.dynamic_slice_in_dim(
                upstream_group, offset, block_rows, 0
            ).reshape(block_rows, queries_per_group, HEAD_SIZE)
            sentence_query = lax.dynamic_slice_in_dim(sentence, offset, block_rows, 0)
            allowed = (sentence[None, :] <= sentence_query[:, None]) & (
                sentence[None, :] >= sentence_query[:, None] - 3
            )
            scores = (
                jnp.einsum("qhd,kd->hqk", query_block, key_head, preferred_element_type=jnp.float32)
                * factor
            )
            raised = jnp.where(allowed[None], jnp.exp(scores), 0.0)
            attend = raised / jnp.sum(raised, axis=-1, keepdims=True)
            rounded = attend.astype(jnp.bfloat16)
            output_block = jnp.einsum(
                "hqk,kd->qhd", rounded, value_head, preferred_element_type=jnp.float32
            ).astype(jnp.bfloat16)
            grad_attend = jnp.einsum(
                "qhd,kd->hqk", upstream_block, value_head, preferred_element_type=jnp.float32
            )
            dscore = (
                attend
                * (grad_attend - jnp.sum(attend * grad_attend, axis=-1, keepdims=True))
                * factor
            ).astype(jnp.bfloat16)
            query_block_grad = jnp.einsum(
                "hqk,kd->qhd", dscore, key_head, preferred_element_type=jnp.float32
            ).astype(jnp.bfloat16)
            key_window_grad = jnp.einsum(
                "hqk,qhd->kd", dscore, query_block, preferred_element_type=jnp.float32
            )
            value_window_grad = jnp.einsum(
                "hqk,qhd->kd", rounded, upstream_block, preferred_element_type=jnp.float32
            )
            output_buf = lax.dynamic_update_slice_in_dim(
                output_buf, output_block.reshape(block_rows, group_cols), offset, 0
            )
            query_buf = lax.dynamic_update_slice_in_dim(
                query_buf, query_block_grad.reshape(block_rows, group_cols), offset, 0
            )
            key_old = key_buf
            key_buf = key_old + key_window_grad
            value_old = value_buf
            value_buf = value_old + value_window_grad
            return (output_buf, query_buf, key_buf, value_buf)

        starting = (
            jnp.zeros((length, group_cols), jnp.bfloat16),
            jnp.zeros((length, group_cols), jnp.bfloat16),
            jnp.zeros((length, HEAD_SIZE), jnp.float32),
            jnp.zeros((length, HEAD_SIZE), jnp.float32),
        )
        output_buf, query_buf, key_buf, value_buf = lax.fori_loop(
            0, block_count, block_step, starting
        )
        output_parts.append(output_buf)
        query_parts.append(query_buf)
        key_parts.append(key_buf.astype(jnp.bfloat16))
        value_parts.append(value_buf.astype(jnp.bfloat16))
    output_all = jnp.concatenate(output_parts, axis=1)
    query_all = jnp.concatenate(query_parts, axis=1)
    key_all = jnp.concatenate(key_parts, axis=1)
    value_all = jnp.concatenate(value_parts, axis=1)
    sliced = cotangent
    proj_grad = lax.psum_scatter(
        lax.dot_general(
            sliced, output_all, (((0,), (0,)), ((), ())), preferred_element_type=jnp.float32
        ),
        ("dp", "fsdp"),
        scatter_dimension=0,
        tiled=True,
    ).astype(jnp.bfloat16)
    query_grad, key_gradient, value_gradient = (
        lax.all_to_all(query_all[None], "seq", split_axis=1, concat_axis=2, tiled=True),
        lax.all_to_all(key_all[None], "seq", split_axis=1, concat_axis=2, tiled=True),
        lax.all_to_all(value_all[None], "seq", split_axis=1, concat_axis=2, tiled=True),
    )
    return (query_grad, key_gradient, value_gradient, proj_grad)


def solution(mesh):
    in_specs = (
        P(("dp", "fsdp"), "seq", None),
        P(("dp", "fsdp"), "seq", None),
        P(("dp", "fsdp"), "seq", None),
        P(("dp", "fsdp"), "seq", None),
        P(("dp", "fsdp"), "seq"),
        P(("dp", "fsdp"), None),
    )
    out_specs = (
        P(("dp", "fsdp"), "seq", None),
        P(("dp", "fsdp"), "seq", None),
        P(("dp", "fsdp"), "seq", None),
        P(("dp", "fsdp"), "seq"),
    )
    return jax.shard_map(
        per_device, mesh=mesh, in_specs=in_specs, out_specs=out_specs, check_vma=False
    )
```

profile of v0, /device:TPU:1, one launch (start us, length us, event | category | flops | bytes accessed | tf_op | source)
XLA Modules:
  0.0 522.7 jit_solution(9837036897079936077)
XLA Ops:
  9.7 2.3 reduce.1
  12.8 3.4 all-to-all-start
  16.7 2.3 reduce.2
  19.7 2.0 all-to-all-done
  21.7 4.1 all-to-all-start.2
  25.8 2.8 copy.318
  28.7 22.4 %reduce = bf16[4096,128]{1,0:T(8,128)(2,1)S(1)} reduce(bf16[4096,1,128]{2,1,0:T(2,128)(2,1)S(1)} %bitcast.229, bf16[]{:T(256)} %broadcast.129), dimensions={1}, to_apply=%bitcast.183.reduce_sub_computation | reduce | bytes 2097154
  51.1 1.1 reshape.207
  52.4 3.6 all-to-all-start.1
  57.0 1.2 reshape.212
  59.0 9.4 %all-to-all-done.1 = bf16[2,2,131072]{2,1,0:T(2,128)(2,1)S(1)} async-done(((bf16[2,2,131072]{2,1,0:T(2,128)(2,1)}), bf16[2,2,131072]{2,1,0:T(2,128)(2,1)S(1)}, u32[]{:S(2)}, u32[]{:S(2)}) %all-to-all-start.1) | async-done | bytes 1048608 | tf_op jit(solution)/shard_map/all_to_all | solution.py:28
  73.9 1.9 convolution_convert_fusion.1
  76.2 1.9 convolution_convert_fusion.4
  78.1 17.5 %convolution_bitcast_fusion = f32[4096,2048]{0,1:T(8,128)} fusion(bf16[1,256,4096]{2,1,0:T(8,128)(2,1)} %all-gather.3.cloned.1.call-done, bf16[256,512]{0,1:T(8,128)(2,1)} %bitcast.290, bf16[256,512]{0,1:T(8,128)(2,1)} %bitcast.289, bf16[256,512]{0,1:T(8,128)(2,1)S(1)} %bitcast.288, bf16[256,512]{0,1:T(8,128)(2,1)} %bitcast.291), kind=kOutput, calls=%fused_computation.4 | convolution fusion | flops 4299161600 | bytes 36700160 | tf_op jit(solution)/shard_map/dot_general | solution.py:125
  95.6 1.5 fusion.70
  97.1 1.4 fusion.68
  98.5 1.4 fusion.66
  99.9 2.5 fusion.80
  102.5 75.4 %all-gather.5.cloned.1.call-done = bf16[4096,2048]{1,0:T(8,128)(2,1)} async-done(((bf16[256,2048]{1,0:T(8,128)(2,1)}), bf16[4096,2048]{1,0:T(8,128)(2,1)}) %all-gather.5.cloned.1.call-update) | async-done | bytes 16777232 | tf_op jit(solution)/shard_map/all_gather | solution.py:24
  177.9 8.4 %convolution_convert_fusion = bf16[256,2048]{1,0:T(8,128)(2,1)S(1)} fusion(bf16[4096,2048]{1,0:T(8,128)(2,1)} %all-gather.5.cloned.1.call-done, bf16[1,256,4096]{2,1,0:T(8,128)(2,1)S(1)} %copy-done), kind=kOutput, calls=%fused_computation.5 | convolution fusion | flops 4295491584 | bytes 19922944 | tf_op jit(solution)/shard_map/dot_general | solution.py:22
  189.1 1.2 convolution_bitcast_fusion.3
  190.3 2.7 fusion.35
  193.0 1.3 convolution_bitcast_fusion.2
  194.4 2.8 fusion.36
  197.2 1.3 convolution_bitcast_fusion.1
  198.5 3.4 fusion.37
  201.9 1.3 convolution_bitcast_fusion.4
  203.3 2.5 fusion.34
  206.2 2.2 reduce.4
  209.4 3.5 all-to-all-start.4
  212.9 2.3 fusion.39
  215.2 2.4 fusion.40
  217.6 2.9 fusion.41
  220.5 3.4 convolution_convert_fusion.7
  223.9 3.5 convolution_convert_fusion.6
  227.4 3.7 convolution_convert_fusion.5
  231.1 2.7 convolution_convert_fusion.8
  235.6 2.2 reduce.5
  238.7 3.7 all-to-all-start.5
  242.6 1.6 copy.423
  244.2 6.8 %reduce.3 = bf16[256,2048]{1,0:T(8,128)(2,1)S(1)} reduce(bf16[256,1,2048]{2,1,0:T(2,128)(2,1)S(1)} %bitcast.228, bf16[]{:T(256)} %broadcast.129), dimensions={1}, to_apply=%bitcast.225.reduce_sub_computation | reduce | bytes 2097154
  251.1 1.6 reshape.213
  252.6 3.6 all-to-all-start.3
  259.0 10.8 %all-to-all-done.3 = bf16[2,2,131072]{2,1,0:T(2,128)(2,1)S(1)} async-done(((bf16[2,2,131072]{2,1,0:T(2,128)(2,1)}), bf16[2,2,131072]{2,1,0:T(2,128)(2,1)S(1)}, u32[]{:S(2)}, u32[]{:S(2)}) %all-to-all-start.3) | async-done | bytes 1048608 | tf_op jit(solution)/shard_map/all_to_all | solution.py:133
  271.9 1.3 copy.372
  273.2 239.3 %reduce-scatter.2.cloned.1.call-done = f32[256,2048]{0,1:T(8,128)} async-done(((f32[4096,2048]{0,1:T(8,128)}), f32[256,2048]{0,1:T(8,128)}) %reduce-scatter.2.cloned.1.call-update) | async-done | bytes 2097168 | tf_op jit(solution)/shard_map/reduce_scatter | solution.py:124
  512.6 1.7 convert_element_type.155
  514.3 1.4 copy.375
  (124 shorter events, 23.7 us)
Async XLA Ops:
  7.2 1.5 copy-start.22
  7.2 70.9 %all-gather.3.cloned.1.call-start = ((), (), s32[]{:S(2)}) async-start(), calls=%async_computation.7 | async-start | bytes 3145728 | tf_op jit(solution)/shard_map/all_gather | solution.py:18
  7.9 8.3 %copy-start.23 = (bf16[1,128,1024]{2,1,0:T(8,128)(2,1)S(1)}, bf16[1,128,1024]{2,1,0:T(8,128)(2,1)}, u32[]{:S(2)}) copy-start(bf16[1,128,1024]{2,1,0:T(8,128)(2,1)} %param.8) | copy-start | bytes 786436
  7.9 170.0 %all-gather.5.cloned.1.call-start = ((), (), s32[]{:S(2)}) async-start(), calls=%async_computation.8 | async-start | bytes 17825792 | tf_op jit(solution)/shard_map/all_gather | solution.py:24
  9.7 16.1 %copy-start.1 = (bf16[1,128,4096]{2,1,0:T(8,128)(2,1)S(1)}, bf16[1,128,4096]{2,1,0:T(8,128)(2,1)}, u32[]{:S(2)}) copy-start(bf16[1,128,4096]{2,1,0:T(8,128)(2,1)} %param.6) | copy-start | bytes 3145732
  12.8 8.9 %all-to-all-start = ((bf16[2,2,32768]{2,1,0:T(2,128)(2,1)}), bf16[2,2,32768]{2,1,0:T(2,128)(2,1)S(1)}, u32[]{:S(2)}, u32[]{:S(2)}) async-start(bf16[2,2,32768]{2,1,0:T(2,128)(2,1)} %reshape.209), calls=%async_computation | async-start | bytes 524288 | tf_op jit(solution)/shard_map/all_to_all | solution.py:29
  21.7 30.7 %all-to-all-start.2 = ((bf16[2,2,32768]{2,1,0:T(2,128)(2,1)}), bf16[2,2,32768]{2,1,0:T(2,128)(2,1)}, u32[]{:S(2)}, u32[]{:S(2)}) async-start(bf16[2,2,32768]{2,1,0:T(2,128)(2,1)} %reshape.211), calls=%async_computation.2 | async-start | bytes 524288 | tf_op jit(solution)/shard_map/all_to_all | solution.py:30
  28.7 23.6 %copy-start.28 = (s32[1,8]{1,0:T(1,128)S(1)}, s32[1,8]{1,0:T(1,128)}, u32[]{:S(2)}) copy-start(s32[1,8]{1,0:T(1,128)} %param.11) | copy-start | bytes 100
  52.4 16.0 %all-to-all-start.1 = ((bf16[2,2,131072]{2,1,0:T(2,128)(2,1)}), bf16[2,2,131072]{2,1,0:T(2,128)(2,1)S(1)}, u32[]{:S(2)}, u32[]{:S(2)}) async-start(bf16[2,2,131072]{2,1,0:T(2,128)(2,1)} %reshape.207), calls=%async_computation.1 | async-start | bytes 2097152 | tf_op jit(solution)/shard_map/all_to_all | solution.py:28
  56.0 456.6 %reduce-scatter.2.cloned.1.call-start = ((), (), s32[]{:S(2)}) async-start(), calls=%async_computation.9 | async-start | bytes 35651584 | tf_op jit(solution)/shard_map/reduce_scatter | solution.py:124
  70.1 1.0 copy-start.20
  70.3 5.6 %copy-start.10 = (bf16[256,512]{0,1:T(8,128)(2,1)}, bf16[256,512]{0,1:T(8,128)(2,1)S(1)}, u32[]{:S(2)}) copy-start(bf16[256,512]{0,1:T(8,128)(2,1)S(1)} %copy.320) | copy-start | bytes 786436
  70.4 28.1 %copy-start.11 = (bf16[256,512]{0,1:T(8,128)(2,1)}, bf16[256,512]{0,1:T(8,128)(2,1)S(1)}, u32[]{:S(2)}) copy-start(bf16[256,512]{0,1:T(8,128)(2,1)S(1)} %copy.337) | copy-start | bytes 786436
  70.6 26.5 %copy-start.13 = (bf16[256,512]{0,1:T(8,128)(2,1)}, bf16[256,512]{0,1:T(8,128)(2,1)S(1)}, u32[]{:S(2)}) copy-start(bf16[256,512]{0,1:T(8,128)(2,1)S(1)} %copy.332) | copy-start | bytes 786436
  70.7 24.9 %copy-start.14 = (bf16[256,512]{0,1:T(8,128)(2,1)}, bf16[256,512]{0,1:T(8,128)(2,1)S(1)}, u32[]{:S(2)}) copy-start(bf16[256,512]{0,1:T(8,128)(2,1)S(1)} %copy.327) | copy-start | bytes 786436
  71.1 1.1 copy-start.6
  72.5 1.1 copy-start.5
  73.9 2.3 copy-start.4
  76.2 1.9 copy-start.21
  99.9 77.9 %copy-start = (bf16[1,256,4096]{2,1,0:T(8,128)(2,1)S(1)}, bf16[1,256,4096]{2,1,0:T(8,128)(2,1)}, u32[]{:S(2)}) copy-start(bf16[1,256,4096]{2,1,0:T(8,128)(2,1)} %all-gather.3.cloned.1.call-done) | copy-start | bytes 6291460
  186.4 3.9 copy-start.15
  189.1 3.9 copy-start.18
  190.3 6.9 %copy-start.7 = (f32[4,256,256]{1,2,0:T(8,128)}, f32[4,256,256]{1,2,0:T(8,128)S(1)}, u32[]{:S(2)}) copy-start(f32[4,256,256]{1,2,0:T(8,128)S(1)} %convolution_bitcast_fusion.3) | copy-start | bytes 3145732
  194.3 7.5 %copy-start.8 = (f32[4,256,256]{1,2,0:T(8,128)}, f32[4,256,256]{1,2,0:T(8,128)S(1)}, u32[]{:S(2)}) copy-start(f32[4,256,256]{1,2,0:T(8,128)S(1)} %convolution_bitcast_fusion.2) | copy-start | bytes 3145732
  198.5 3.4 copy-start.9
  201.9 3.8 copy-start.27
  203.3 9.6 %copy-start.19 = (bf16[256,512]{0,1:T(8,128)(2,1)S(1)}, bf16[256,512]{0,1:T(8,128)(2,1)}, u32[]{:S(2)}) copy-start(bf16[256,512]{0,1:T(8,128)(2,1)} %copy-done.18) | copy-start | bytes 786436
  209.4 29.4 %all-to-all-start.4 = ((bf16[2,2,32768]{2,1,0:T(2,128)(2,1)}), bf16[2,2,32768]{2,1,0:T(2,128)(2,1)S(1)}, u32[]{:S(2)}, u32[]{:S(2)}) async-start(bf16[2,2,32768]{2,1,0:T(2,128)(2,1)} %reshape.215), calls=%async_computation.4 | async-start | bytes 524288 | tf_op jit(solution)/shard_map/all_to_all | solution.py:134
  212.9 2.3 copy-start.17
  215.2 2.4 copy-start.16
  223.9 9.9 %copy-start.12 = (bf16[256,512]{0,1:T(8,128)(2,1)S(1)}, bf16[256,512]{0,1:T(8,128)(2,1)}, u32[]{:S(2)}) copy-start(bf16[256,512]{0,1:T(8,128)(2,1)} %copy.418) | copy-start | bytes 786436
  233.8 1.0 copy-start.24
  233.8 1.1 copy-start.25
  234.2 0.9 copy-start.26
  238.7 3.7 copy-start.2
  238.7 13.9 %all-to-all-start.5 = ((bf16[2,2,32768]{2,1,0:T(2,128)(2,1)}), bf16[2,2,32768]{2,1,0:T(2,128)(2,1)S(1)}, u32[]{:S(2)}, u32[]{:S(2)}) async-start(bf16[2,2,32768]{2,1,0:T(2,128)(2,1)} %reshape.217), calls=%async_computation.5 | async-start | bytes 524288 | tf_op jit(solution)/shard_map/all_to_all | solution.py:135
  251.0 5.2 copy-start.3
  252.6 17.1 %all-to-all-start.3 = ((bf16[2,2,131072]{2,1,0:T(2,128)(2,1)}), bf16[2,2,131072]{2,1,0:T(2,128)(2,1)S(1)}, u32[]{:S(2)}, u32[]{:S(2)}) async-start(bf16[2,2,131072]{2,1,0:T(2,128)(2,1)} %reshape.213), calls=%async_computation.3 | async-start | bytes 2097152 | tf_op jit(solution)/shard_map/all_to_all | solution.py:133
Sparse Core Ops, SparseCore 0:
  9.6 38.3 all-gather.2
  50.1 127.6 all-gather.4
  182.1 330.4 reduce-scatter.1
where the time goes:
time: 531 us; the launch traced here: 523 us
  waiting for transfers between devices  338 us (64%)
  matrix products  77.8 us (15%)
  other arithmetic  40.6 us (8%)
  local copies, waits for them, and re-layouts  28.8 us (5%)
  starting transfers between devices  22.2 us (4%)
  between operations  15 us (3%)
    reduce_scatter x1, waiting for transfers between devices, per_device(): lax.psum_scatter(lax.dot_general(sliced, output_all, (((0,), (0,)), ((),...  239 us
    all_gather x1, waiting for transfers between devices, per_device(): lax.all_gather(proj_weight, ('dp', 'fsdp'), axis=0, tiled=True)  75.4 us
    unnamed x6, other arithmetic  38.4 us
    unnamed x84, local copies, waits for them, and re-layouts  19.8 us
    dot_general x1, matrix products, per_device(): lax.dot_general(sliced, output_all, (((0,), (0,)), ((), ())), preferred_e...  17.5 us
    dot_general x4, matrix products, block_step(): jnp.einsum('hqk,kd->qhd', dscore, key_head, preferred_element_type=jnp.fl...  13.3 us
    dot_general x4, matrix products, block_step(): jnp.einsum('hqk,qhd->kd', dscore, query_block, preferred_element_type=jnp...  11.3 us
    all_to_all x1, waiting for transfers between devices, per_device(): lax.all_to_all(query_all[None], 'seq', split_axis=1, concat_axis=2, tiled...  10.8 us
  transfers between devices with their start and end apart: 9, of which 5 were waited for; matrix products, arithmetic and copies ran while one was open for 27% of the time, Pallas kernels for 0%

commit v1 on v0

--- a/solution.py
+++ b/solution.py
@@ -3,11 +3,18 @@
 import jax
 import jax.numpy as jnp
 from jax import lax
+from jax.experimental import pallas as pl
+from jax.experimental.pallas import tpu as pltpu
 from jax.sharding import PartitionSpec as P
 
 QUERY_HEADS = 32
 KEY_VALUE_HEADS = 8
 HEAD_SIZE = 128
+
+
+def running_sums(lengths):
+    index = jnp.arange(lengths.shape[0], dtype=jnp.int32)
+    return jnp.sum(jnp.where(index[None, :] <= index[:, None], lengths[None, :], 0), axis=1)
 
 
 def per_device(
@@ -32,7 +39,7 @@
     heads_of_queries = heads_of_queries[0]
     heads_of_keys = heads_of_keys[0]
     heads_of_values = heads_of_values[0]
-    bounds = jnp.cumsum(sent_lengths[0])
+    bounds = running_sums(sent_lengths[0])
     places = jnp.arange(length, dtype=jnp.int32)
     sentence = jnp.sum((places[:, None] >= bounds[None, :]).astype(jnp.int32), axis=1)
     block_rows = min(512, length)
@@ -137,6 +144,501 @@
     return (query_grad, key_gradient, value_gradient, proj_grad)
 
 
+MESH = pl.DeviceIdType.MESH
+GROUP = QUERY_HEADS // KEY_VALUE_HEADS
+GROUP_COLS = GROUP * HEAD_SIZE
+
+
+def heads_kernel(
+    q_in, k_in, v_in, cot_in, w_in, sid_in,
+    dq_out, dk_out, dv_out, proj_out,
+    cot, qg, kg, vg, sidg, wg, att, outb, acc, part, from_below, from_above, dqb, dkb, dvb,
+    loc_sem, sid_s, sid_r, qkv_s, qkv_r, wp_s, wp_r, wu_s, wu_r, wd_s, wd_r,
+    cot_s, cot_r, red_s, up_r, down_r, fin_s, fin_r, ret_s, ret_r,
+):
+    s = lax.axis_index("seq")
+    d = lax.axis_index("dp")
+    f = lax.axis_index("fsdp")
+    length = qg.shape[0] // 4
+    half = length // 2
+    block = cot.shape[2]
+    piece = block // 4
+    factor = 1.0 / math.sqrt(HEAD_SIZE)
+
+    def rows_of(side, window):
+        return pl.ds(pl.multiple_of(window * length + side * half, half), half)
+
+    def cols(index, width):
+        return pl.ds(pl.multiple_of(index * width, width), width)
+
+    def other(i):
+        return lax.rem(f + i, 4)
+
+    def source(i):
+        return lax.rem(f + 4 - i, 4)
+
+    def side(t):
+        return s if t == 0 else 1 - s
+
+    def remote(src, dst, send, recv, device):
+        return pltpu.make_async_remote_copy(
+            src_ref=src, dst_ref=dst, send_sem=send, recv_sem=recv,
+            device_id=device, device_id_type=MESH,
+        )
+
+    pairs = [(t, i) for i in range(4) for t in range(2) if (t, i) != (0, 0)]
+    beside = (1 - s, d, f)
+
+    barrier = pltpu.get_barrier_semaphore()
+    for t, i in pairs:
+        pl.semaphore_signal(
+            barrier, inc=1, device_id=(side(t), d, other(i)), device_id_type=MESH
+        )
+
+    @pl.when(d > 0)
+    def _():
+        pl.semaphore_signal(barrier, inc=1, device_id=(s, d - 1, f), device_id_type=MESH)
+
+    @pl.when(d < 3)
+    def _():
+        pl.semaphore_signal(barrier, inc=1, device_id=(s, d + 1, f), device_id_type=MESH)
+
+    pl.semaphore_wait(barrier, 8 + d * (3 - d) // 2)
+
+    def weight_rows(plane, window):
+        return pl.ds(pl.multiple_of((plane * 4 + window) * piece, piece), piece)
+
+    def weight_copy(i, target, origin):
+        return remote(
+            w_in.at[:, cols(target, GROUP_COLS)], wg.at[weight_rows(d, origin)],
+            wp_s.at[i], wp_r.at[i], (s, d, target),
+        )
+
+    for i in (1, 2, 3):
+        weight_copy(i, other(i), f).start()
+    own_weight = pltpu.make_async_copy(
+        w_in.at[:, cols(f, GROUP_COLS)], wg.at[weight_rows(d, f)], loc_sem.at[0]
+    )
+    own_weight.start()
+
+    def sid_copy(i, target, origin):
+        return remote(sid_in, sidg.at[origin], sid_s.at[i], sid_r.at[i], (s, d, target))
+
+    def own_or_sent(a, to_side, to_window, from_side, from_window):
+        head = to_side * 4 + to_window
+        src, dst, width = ((q_in, qg, GROUP_COLS), (k_in, kg, HEAD_SIZE), (v_in, vg, HEAD_SIZE))[a]
+        return src.at[0, :, cols(head, width)], dst.at[rows_of(from_side, from_window)]
+
+    def qkv_copy(a, t, i):
+        src, dst = own_or_sent(a, side(t), other(i), s, f)
+        return remote(src, dst, qkv_s.at[a, t, i], qkv_r.at[a, t, i], (side(t), d, other(i)))
+
+    def qkv_arrival(a, t, i):
+        src, dst = own_or_sent(a, s, f, side(t), source(i))
+        return remote(src, dst, qkv_s.at[a, t, i], qkv_r.at[a, t, i], beside)
+
+    local_copies = []
+    for a in range(3):
+        src, dst = own_or_sent(a, s, f, s, f)
+        local_copies.append(pltpu.make_async_copy(src, dst, loc_sem.at[1 + a]))
+    local_copies.append(pltpu.make_async_copy(sid_in, sidg.at[f], loc_sem.at[4]))
+    for copy in local_copies:
+        copy.start()
+    for i in (1, 2, 3):
+        sid_copy(i, other(i), f).start()
+    for t, i in pairs:
+        for a in range(3):
+            qkv_copy(a, t, i).start()
+
+    fy = lax.rem(f + 2, 4)
+    fc = f + 1 - 2 * lax.rem(f, 2)
+    fcy = lax.rem(fc + 2, 4)
+    to_x, to_y, to_core = (1 - s, d, f), (s, d, fy), (s, d, fc)
+    order = (3 * (1 - d // 2), lax.rem(12 - 2 * d, 5), 1 + lax.rem(d, 2), d)
+
+    def span(from_side, window, part_of):
+        start = window * length + from_side * half
+        if part_of is None:
+            return pl.ds(pl.multiple_of(start, half), half)
+        quarter = half // 2
+        return pl.ds(pl.multiple_of(start + part_of * quarter, quarter), quarter)
+
+    kinds = (
+        (to_x, (s, f, None), (1 - s, f, None)),
+        (to_y, (s, f, None), (s, fy, None)),
+        (to_core, (s, f, None), (s, fc, None)),
+        (to_y, (1 - s, f, 0), (1 - s, fy, 0)),
+        (to_core, (1 - s, f, None), (1 - s, fc, None)),
+        (to_x, (s, fy, 1), (1 - s, fy, 1)),
+        (to_core, (s, fy, None), (s, fcy, None)),
+        (to_core, (1 - s, fy, 0), (1 - s, fcy, 0)),
+        (to_core, (1 - s, fy, 1), (1 - s, fcy, 1)),
+    )
+
+    def cot_copy(j, kind):
+        device, sent, _ = kinds[kind]
+        dst = cot.at[order[j], span(*sent)]
+        src = cot_in.at[0, :, cols(order[j], block)] if kind < 3 else dst
+        return remote(src, dst, cot_s.at[kind, j], cot_r.at[kind, j], device)
+
+    def cot_arrival(j, kind):
+        device, _, came = kinds[kind]
+        dst = cot.at[order[j], span(*came)]
+        return remote(dst, dst, cot_s.at[kind, j], cot_r.at[kind, j], device)
+
+    def own_cot(j):
+        return pltpu.make_async_copy(
+            cot_in.at[0, :, cols(order[j], block)], cot.at[order[j], span(s, f, None)],
+            loc_sem.at[5 + j],
+        )
+
+    def cot_send(j):
+        for kind in (0, 1, 2):
+            cot_copy(j, kind).start()
+        own_cot(j).start()
+
+    def cot_pass(j):
+        cot_arrival(j, 0).wait_recv()
+        cot_copy(j, 3).start()
+        cot_copy(j, 4).start()
+        cot_arrival(j, 1).wait_recv()
+        cot_copy(j, 5).start()
+        cot_copy(j, 6).start()
+
+    def cot_pass_on(j):
+        cot_arrival(j, 3).wait_recv()
+        cot_copy(j, 7).start()
+        cot_arrival(j, 5).wait_recv()
+        cot_copy(j, 8).start()
+
+    def cot_ready(j):
+        for kind in (2, 4, 6, 7, 8):
+            cot_arrival(j, kind).wait_recv()
+        own_cot(j).wait()
+
+    def plane_rows(plane):
+        return pl.ds(pl.multiple_of(plane * block, block), block)
+
+    def weight_up(plane):
+        ref = wg.at[plane_rows(plane)]
+        return remote(ref, ref, wu_s.at[plane], wu_r.at[plane], (s, d + 1, f))
+
+    def weight_down(plane):
+        ref = wg.at[plane_rows(plane)]
+        return remote(ref, ref, wd_s.at[plane], wd_r.at[plane], (s, d - 1, f))
+
+    def weight_step(k):
+        if k:
+            @pl.when(d >= k)
+            def _():
+                weight_up(d - k).wait_recv()
+
+        @pl.when((d >= k) & (d < 3))
+        def _():
+            weight_up(d - k).start()
+
+        if k:
+            @pl.when(d + k <= 3)
+            def _():
+                weight_down(d + k).wait_recv()
+
+        @pl.when((d + k <= 3) & (d > 0))
+        def _():
+            weight_down(d + k).start()
+
+    def forward(i, carry):
+        window = lax.rem(f + 4 - i, 4)
+        for a in range(3):
+            @pl.when(i > 0)
+            def _():
+                qkv_arrival(a, 0, i).wait_recv()
+
+            qkv_arrival(a, 1, i).wait_recv()
+
+        @pl.when(i > 0)
+        def _():
+            sid_copy(i, fc, source(i)).wait_recv()
+
+        rows = pl.ds(pl.multiple_of(window * length, length), length)
+        keys = kg[rows, :]
+        values = vg[rows, :]
+        sent_key = jnp.broadcast_to(sidg[window][0:1, :], (length, length))
+        sent_query = sent_key.T
+        allowed = (sent_key <= sent_query) & (sent_key >= sent_query - 3.0)
+        for h in range(GROUP):
+            here = slice(h * HEAD_SIZE, (h + 1) * HEAD_SIZE)
+            scores = factor * lax.dot_general(
+                qg[rows, here], keys, (((1,), (1,)), ((), ())), preferred_element_type=jnp.float32
+            )
+            raised = jnp.where(allowed, jnp.exp(scores), 0.0)
+            attend = raised * (1.0 / jnp.sum(raised, axis=1, keepdims=True))
+            att[window * GROUP + h] = attend
+            outb[rows, here] = jnp.dot(
+                attend.astype(jnp.bfloat16), values, preferred_element_type=jnp.float32
+            ).astype(jnp.bfloat16)
+        return carry
+
+    def slot_copy_up(slot):
+        return remote(
+            part.at[slot], from_below.at[slot], red_s.at[slot], up_r.at[slot], (s, d + 1, f)
+        )
+
+    def slot_copy_down(slot):
+        return remote(
+            part.at[slot], from_above.at[slot], red_s.at[slot], down_r.at[slot], (s, d - 1, f)
+        )
+
+    def final_copy(i, target, origin):
+        return remote(
+            part.at[d * 4 + target], proj_out.at[:, cols(origin, GROUP_COLS)],
+            fin_s.at[i], fin_r.at[i], (s, d, target),
+        )
+
+    def own_final():
+        return pltpu.make_async_copy(
+            part.at[d * 4 + f], proj_out.at[:, cols(f, GROUP_COLS)], loc_sem.at[9]
+        )
+
+    def reduce_step(j):
+        plane = order[j]
+
+        def one(i, carry):
+            r = lax.rem(f + i, 4)
+            slot = plane * 4 + r
+            acc[...] = lax.dot_general(
+                cot[plane, :, cols(r, piece)], outb[...],
+                (((0,), (0,)), ((), ())), preferred_element_type=jnp.float32,
+            )
+
+            @pl.when((plane >= d) & (d > 0))
+            def _():
+                slot_copy_up(slot).wait_recv()
+                acc[...] += from_below[slot].astype(jnp.float32)
+
+            @pl.when((plane <= d) & (d < 3))
+            def _():
+                slot_copy_down(slot).wait_recv()
+                acc[...] += from_above[slot].astype(jnp.float32)
+
+            part[slot] = acc[...].astype(jnp.bfloat16)
+            if j < 3:
+                @pl.when(plane > d)
+                def _():
+                    slot_copy_up(slot).start()
+
+                @pl.when(plane < d)
+                def _():
+                    slot_copy_down(slot).start()
+            else:
+                @pl.when(i > 0)
+                def _():
+                    final_copy(i, r, f).start()
+
+                @pl.when(i == 0)
+                def _():
+                    own_final().start()
+            return carry
+
+        lax.fori_loop(0, 4, one, 0)
+
+    returned = ((dqb, dq_out, GROUP_COLS), (dkb, dk_out, HEAD_SIZE), (dvb, dv_out, HEAD_SIZE))
+
+    def return_copy(a, t, i):
+        buffer, out, width = returned[a]
+        window = lax.rem(f + i, 4)
+        return remote(
+            buffer.at[rows_of(side(t), window)], out.at[0, :, cols(s * 4 + f, width)],
+            ret_s.at[a, t, i], ret_r.at[a, t, i], (side(t), d, window),
+        )
+
+    def return_arrival(a, t, i):
+        buffer, out, width = returned[a]
+        return remote(
+            buffer.at[rows_of(s, f)], out.at[0, :, cols(side(t) * 4 + source(i), width)],
+            ret_s.at[a, t, i], ret_r.at[a, t, i], beside,
+        )
+
+    def own_return(a):
+        buffer, out, width = returned[a]
+        return pltpu.make_async_copy(
+            buffer.at[rows_of(s, f)], out.at[0, :, cols(s * 4 + f, width)], loc_sem.at[10 + a]
+        )
+
+    def backward(i, carry):
+        window = lax.rem(f + i, 4)
+        rows = pl.ds(pl.multiple_of(window * length, length), length)
+        upstream = jnp.zeros((length, GROUP_COLS), jnp.float32)
+        for plane in range(4):
+            upstream = upstream + jnp.dot(
+                cot[plane, rows, :], wg[plane * block : (plane + 1) * block, :],
+                preferred_element_type=jnp.float32,
+            )
+        upstream = upstream.astype(jnp.bfloat16)
+        keys = kg[rows, :]
+        values = vg[rows, :]
+        key_sum = jnp.zeros((length, HEAD_SIZE), jnp.float32)
+        value_sum = jnp.zeros((length, HEAD_SIZE), jnp.float32)
+        for h in range(GROUP):
+            here = slice(h * HEAD_SIZE, (h + 1) * HEAD_SIZE)
+            attend = att[window * GROUP + h]
+            upstream_head = upstream[:, here]
+            grad_attend = lax.dot_general(
+                upstream_head, values, (((1,), (1,)), ((), ())), preferred_element_type=jnp.float32
+            )
+            mean = jnp.sum(attend * grad_attend, axis=1, keepdims=True)
+            dscore = (attend * (grad_attend - mean) * factor).astype(jnp.bfloat16)
+            dqb[rows, here] = jnp.dot(
+                dscore, keys, preferred_element_type=jnp.float32
+            ).astype(jnp.bfloat16)
+            key_sum = key_sum + lax.dot_general(
+                dscore, qg[rows, here], (((0,), (0,)), ((), ())),
+                preferred_element_type=jnp.float32,
+            )
+            value_sum = value_sum + lax.dot_general(
+                attend.astype(jnp.bfloat16), upstream_head, (((0,), (0,)), ((), ())),
+                preferred_element_type=jnp.float32,
+            )
+        dkb[rows, :] = key_sum.astype(jnp.bfloat16)
+        dvb[rows, :] = value_sum.astype(jnp.bfloat16)
+        for a in range(3):
+            @pl.when(i > 0)
+            def _():
+                return_copy(a, 0, i).start()
+
+            @pl.when(i == 0)
+            def _():
+                own_return(a).start()
+
+            return_copy(a, 1, i).start()
+        return carry
+
+    own_weight.wait()
+    for i in (1, 2, 3):
+        weight_copy(i, fc, source(i)).wait_recv()
+    weight_step(0)
+    cot_send(0)
+    cot_send(1)
+    for copy in local_copies:
+        copy.wait()
+    lax.fori_loop(0, 4, forward, 0)
+    cot_pass(0)
+    cot_send(2)
+    cot_pass_on(0)
+    cot_pass(1)
+    cot_ready(0)
+    reduce_step(0)
+    weight_step(1)
+    cot_send(3)
+    cot_pass_on(1)
+    cot_pass(2)
+    cot_ready(1)
+    reduce_step(1)
+    cot_pass_on(2)
+    cot_pass(3)
+    cot_ready(2)
+    weight_step(2)
+    reduce_step(2)
+    cot_pass_on(3)
+    cot_ready(3)
+
+    @pl.when(d == 3)
+    def _():
+        weight_up(0).wait_recv()
+
+    @pl.when(d == 0)
+    def _():
+        weight_down(3).wait_recv()
+
+    lax.fori_loop(0, 4, backward, 0)
+    reduce_step(3)
+
+    for i in (1, 2, 3):
+        weight_copy(i, other(i), f).wait_send()
+        sid_copy(i, other(i), f).wait_send()
+        final_copy(i, other(i), f).wait_send()
+        final_copy(i, other(i), source(i)).wait_recv()
+    own_final().wait()
+    for a in range(3):
+        own_return(a).wait()
+        for t, i in pairs:
+            qkv_copy(a, t, i).wait_send()
+            return_copy(a, t, i).wait_send()
+            return_arrival(a, t, i).wait_recv()
+    for j in range(4):
+        for kind in range(9):
+            cot_copy(j, kind).wait_send()
+    for k in range(3):
+        @pl.when((d >= k) & (d < 3))
+        def _():
+            weight_up(d - k).wait_send()
+
+        @pl.when((d + k <= 3) & (d > 0))
+        def _():
+            weight_down(d + k).wait_send()
+    for j in range(3):
+        def drain(i, carry):
+            slot_copy_up(order[j] * 4 + lax.rem(f + i, 4)).wait_send()
+            return carry
+
+        lax.fori_loop(0, 4, drain, 0)
+
+
+def per_device_heads(
+    query_rows, forward_key_rows, forward_value_rows, out_cotangent, proj_weight, sent_lengths
+):
+    half, width = query_rows.shape[1:]
+    length = 2 * half
+    depth = proj_weight.shape[0]
+    bounds = running_sums(sent_lengths[0])
+    places = jnp.arange(length, dtype=jnp.int32)
+    sentence = jnp.sum((places[None, :] >= bounds[:, None]).astype(jnp.float32), axis=0)
+    sentence = jnp.broadcast_to(sentence[None, :], (8, length))
+    block = out_cotangent.shape[2] // 4
+    tokens = 4 * length
+    bf16, f32 = jnp.bfloat16, jnp.float32
+    dma = pltpu.SemaphoreType.DMA
+    return pl.pallas_call(
+        heads_kernel,
+        out_shape=(
+            jax.ShapeDtypeStruct(query_rows.shape, bf16),
+            jax.ShapeDtypeStruct(forward_key_rows.shape, bf16),
+            jax.ShapeDtypeStruct(forward_value_rows.shape, bf16),
+            jax.ShapeDtypeStruct(proj_weight.shape, bf16),
+        ),
+        in_specs=[pl.BlockSpec(memory_space=pl.ANY)] * 6,
+        out_specs=(pl.BlockSpec(memory_space=pl.ANY),) * 4,
+        scratch_shapes=[
+            pltpu.VMEM((4, tokens, block), bf16),
+            pltpu.VMEM((tokens, GROUP_COLS), bf16),
+            pltpu.VMEM((tokens, HEAD_SIZE), bf16),
+            pltpu.VMEM((tokens, HEAD_SIZE), bf16),
+            pltpu.VMEM((4, 8, length), f32),
+            pltpu.VMEM((16 * depth, GROUP_COLS), bf16),
+            pltpu.VMEM((4 * GROUP, length, length), f32),
+            pltpu.VMEM((tokens, GROUP_COLS), bf16),
+            pltpu.VMEM((depth, GROUP_COLS), f32),
+            pltpu.VMEM((16, depth, GROUP_COLS), bf16),
+            pltpu.VMEM((16, depth, GROUP_COLS), bf16),
+            pltpu.VMEM((16, depth, GROUP_COLS), bf16),
+            pltpu.VMEM((tokens, GROUP_COLS), bf16),
+            pltpu.VMEM((tokens, HEAD_SIZE), bf16),
+            pltpu.VMEM((tokens, HEAD_SIZE), bf16),
+            dma((13,)),
+            dma((4,)), dma((4,)),
+            dma((3, 2, 4)), dma((3, 2, 4)),
+            dma((4,)), dma((4,)),
+            dma((4,)), dma((4,)), dma((4,)), dma((4,)),
+            dma((9, 4)), dma((9, 4)),
+            dma((16,)), dma((16,)), dma((16,)),
+            dma((4,)), dma((4,)),
+            dma((3, 2, 4)), dma((3, 2, 4)),
+        ],
+        compiler_params=pltpu.CompilerParams(
+            collective_id=0, has_side_effects=True, vmem_limit_bytes=56 * 1024 * 1024
+        ),
+    )(query_rows, forward_key_rows, forward_value_rows, out_cotangent, proj_weight, sentence)
+
+
 def solution(mesh):
     in_specs = (
         P(("dp", "fsdp"), "seq", None),
@@ -152,6 +654,9 @@
         P(("dp", "fsdp"), "seq", None),
         P(("dp", "fsdp"), "seq"),
     )
+    body = per_device
+    if mesh.shape["seq"] == 2 and mesh.shape["dp"] == 4 and mesh.shape["fsdp"] == 4:
+        body = per_device_heads
     return jax.shard_map(
-        per_device, mesh=mesh, in_specs=in_specs, out_specs=out_specs, check_vma=False
+        body, mesh=mesh, in_specs=in_specs, out_specs=out_specs, check_vma=False
     )

time: 531 us -> 189 us (0.36); the launches traced: 523 us -> 189 us
  waiting for transfers between devices: 338 us -> 0 us
  Pallas kernels: 0 us -> 181 us
  matrix products: 77.8 us -> 0 us
  other arithmetic: 40.6 us -> 0.2 us
  local copies, waits for them, and re-layouts: 28.8 us -> 6.37 us
  starting transfers between devices: 22.2 us -> 0 us
  between operations: 15 us -> 0.67 us
    reduce_scatter x1 -> x0, waiting for transfers between devices: 239 us -> none  [per_device(): lax.psum_scatter(lax.dot_general(sliced, output_all, (((0,), (0,)), ((),...]
    pallas_call x0 -> x1, Pallas kernels: none -> 181 us  [per_device_heads(): pl.pallas_call(heads_kernel, out_shape=(jax.ShapeDtypeStruct(query_rows.s...]
    all_gather x2 -> x0, waiting for transfers between devices: 75.4 us -> none  [the longest x1 75.4 us: per_device(): lax.all_gather(proj_weight, ('dp', 'fsdp'), axis=0, tiled=True)]
    dot_general x26 -> x0, matrix products: 71 us -> none  [the longest x1 17.5 us: per_device(): lax.dot_general(sliced, output_all, (((0,), (0,)), ((), ())), preferred_e...]
    unnamed x6 -> x0, other arithmetic: 38.4 us -> none
    all_to_all x6 -> x0, waiting for transfers between devices: 22.2 us -> none  [the longest x1 10.8 us: per_device(): lax.all_to_all(query_all[None], 'seq', split_axis=1, concat_axis=2, tiled...]
    all_to_all x6 -> x0, starting transfers between devices: 21.9 us -> none  [the longest x1 4.1 us: per_device(): lax.all_to_all(forward_value_rows, 'seq', split_axis=2, concat_axis=1, ti...]
    unnamed x84 -> x12, local copies, waits for them, and re-layouts: 19.8 us -> 5.76 us
  transfers between devices with their start and end apart: 9 -> 0, of which waited for: 5 -> 0; matrix products, arithmetic and copies ran while one was open for 27% -> 0% of each run, Pallas kernels for 0% -> 0%
where the time goes in v1:
time: 189 us
  Pallas kernels  181 us (96%)
  local copies, waits for them, and re-layouts  6.37 us (3%)
    pallas_call x1, Pallas kernels, per_device_heads(): pl.pallas_call(heads_kernel, out_shape=(jax.ShapeDtypeStruct(query_rows.s...  181 us
    unnamed x12, local copies, waits for them, and re-layouts  5.76 us

profile of v1, /device:TPU:1, one launch (start us, length us, event | category | flops | bytes accessed | tf_op | source)
XLA Modules:
  0.0 188.7 jit_solution(13383111622050950114)
XLA Ops:
  0.6 0.0 copy-start.3
  0.6 0.6 copy-done.3
  1.3 0.1 select_reduce_fusion
  1.4 0.1 convert_reduce_fusion
  1.5 0.6 broadcast_in_dim.27.sid_in
  2.1 181.4 %shard_map.93 = (bf16[1,128,4096]{2,1,0:T(8,128)(2,1)}, bf16[1,128,1024]{2,1,0:T(8,128)(2,1)}, bf16[1,128,1024]{2,1,0:T(8,128)(2,1)}, bf16[256,2048]{1,0:T(8,128)(2,1)}) custom-call(bf16[1,128,4096]{2,1,0:T(8,128)(2,1)} %q_in.1, bf16[1,128,1024]{2,1,0:T(8,128)(2,1)} %k_in.1, bf16[1,128,1024]{2,1,0:T(8,128)(2,1)} %v_in.1, bf16[1,128,4096]{2,1,0:T(8,128)(2,1)} %cot_in.1, ...), custom_call_target="tpu_custom_call" | custom-call | tf_op jit(solution)/shard_map/pallas_call | solution.py:600
  183.5 0.0 copy-start.2
  183.5 0.0 copy-start
  183.6 2.4 %copy.14 = bf16[1,128,4096]{2,1,0:T(8,128)(2,1)} copy(bf16[1,128,4096]{2,1,0:T(8,128)(2,1)} %get-tuple-element.8) | data formatting | bytes 2097152
  185.9 0.0 copy-done.2
  185.9 0.0 copy-start.1
  186.0 0.7 copy.15
  186.7 0.3 copy-done.1
  187.0 0.7 copy.16
  187.7 0.0 copy-done
  187.7 1.0 copy.17
Async XLA Ops:
  0.6 0.7 copy-start.3
  183.5 2.4 %copy-start.2 = (bf16[1,128,1024]{2,1,0:T(8,128)(2,1)S(1)}, bf16[1,128,1024]{2,1,0:T(8,128)(2,1)}, u32[]{:S(2)}) copy-start(bf16[1,128,1024]{2,1,0:T(8,128)(2,1)} %get-tuple-element.9) | copy-start | bytes 786436
  183.5 4.2 %copy-start = (bf16[256,2048]{1,0:T(8,128)(2,1)S(1)}, bf16[256,2048]{1,0:T(8,128)(2,1)}, u32[]{:S(2)}) copy-start(bf16[256,2048]{1,0:T(8,128)(2,1)} %get-tuple-element.11) | copy-start | bytes 3145732
  185.9 1.0 copy-start.1

commit v2 on v1

--- a/solution.py
+++ b/solution.py
@@ -518,27 +518,26 @@
     weight_step(0)
     cot_send(0)
     cot_send(1)
-    for copy in local_copies:
-        copy.wait()
+    for copy in local_copies: copy.wait()
     lax.fori_loop(0, 4, forward, 0)
     cot_pass(0)
     cot_send(2)
+    cot_pass(1)
     cot_pass_on(0)
-    cot_pass(1)
+    weight_step(1)
+    cot_send(3)
     cot_ready(0)
     reduce_step(0)
-    weight_step(1)
-    cot_send(3)
     cot_pass_on(1)
     cot_pass(2)
     cot_ready(1)
-    reduce_step(1)
+    weight_step(2)
     cot_pass_on(2)
     cot_pass(3)
+    cot_pass_on(3)
+    reduce_step(1)
     cot_ready(2)
-    weight_step(2)
     reduce_step(2)
-    cot_pass_on(3)
     cot_ready(3)
 
     @pl.when(d == 3)

time: 189 us -> 144 us (0.76)
  Pallas kernels: 181 us -> 137 us
    pallas_call x1, Pallas kernels: 181 us -> 137 us  [per_device_heads(): pl.pallas_call(heads_kernel, out_shape=(jax.ShapeDtypeStruct(query_rows.s...]
where the time goes in v2:
time: 144 us
  Pallas kernels  137 us (95%)
  local copies, waits for them, and re-layouts  6.37 us (4%)
    pallas_call x1, Pallas kernels, per_device_heads(): pl.pallas_call(heads_kernel, out_shape=(jax.ShapeDtypeStruct(query_rows.s...  137 us
    unnamed x12, local copies, waits for them, and re-layouts  5.76 us

profile of v2, /device:TPU:1, one launch (start us, length us, event | category | flops | bytes accessed | tf_op | source)
XLA Modules:
  0.0 144.0 jit_solution(1132076236584832982)
XLA Ops:
  0.6 0.0 copy-start.3
  0.6 0.6 copy-done.3
  1.3 0.1 select_reduce_fusion
  1.4 0.1 convert_reduce_fusion
  1.5 0.6 broadcast_in_dim.27.sid_in
  2.1 136.8 %shard_map.93 = (bf16[1,128,4096]{2,1,0:T(8,128)(2,1)}, bf16[1,128,1024]{2,1,0:T(8,128)(2,1)}, bf16[1,128,1024]{2,1,0:T(8,128)(2,1)}, bf16[256,2048]{1,0:T(8,128)(2,1)}) custom-call(bf16[1,128,4096]{2,1,0:T(8,128)(2,1)} %q_in.1, bf16[1,128,1024]{2,1,0:T(8,128)(2,1)} %k_in.1, bf16[1,128,1024]{2,1,0:T(8,128)(2,1)} %v_in.1, bf16[1,128,4096]{2,1,0:T(8,128)(2,1)} %cot_in.1, ...), custom_call_target="tpu_custom_call" | custom-call | tf_op jit(solution)/shard_map/pallas_call | solution.py:599
  138.9 0.0 copy-start.2
  138.9 0.0 copy-start
  138.9 2.4 %copy.14 = bf16[1,128,4096]{2,1,0:T(8,128)(2,1)} copy(bf16[1,128,4096]{2,1,0:T(8,128)(2,1)} %get-tuple-element.8) | data formatting | bytes 2097152
  141.3 0.0 copy-done.2
  141.3 0.0 copy-start.1
  141.3 0.7 copy.15
  142.0 0.3 copy-done.1
  142.4 0.7 copy.16
  143.1 0.0 copy-done
  143.1 1.0 copy.17
Async XLA Ops:
  0.6 0.7 copy-start.3
  138.9 2.4 %copy-start.2 = (bf16[1,128,1024]{2,1,0:T(8,128)(2,1)S(1)}, bf16[1,128,1024]{2,1,0:T(8,128)(2,1)}, u32[]{:S(2)}) copy-start(bf16[1,128,1024]{2,1,0:T(8,128)(2,1)} %get-tuple-element.9) | copy-start | bytes 786436
  138.9 4.2 %copy-start = (bf16[256,2048]{1,0:T(8,128)(2,1)S(1)}, bf16[256,2048]{1,0:T(8,128)(2,1)}, u32[]{:S(2)}) copy-start(bf16[256,2048]{1,0:T(8,128)(2,1)} %get-tuple-element.11) | copy-start | bytes 3145732
  141.3 1.0 copy-start.1
